TPU v7x, 32 devices: a whole 2x2x4 slice. The times are simulated.
32 devices in a mesh: pb: 4 (over z), ka: 4 (over y, core), ha: 2 (over x).
Axes of the slice: x: 2, y: 2, z: 4, core: 2. Of those that a mesh axis runs over, the one named last changes fastest.
Arguments:
- queries: bfloat16 [4096, 4096], P('pb', 'ha'), may hold values from -512 to 512
- keys: bfloat16 [8, 4, 128, 512], P('pb', 'ka', None, 'ha'), may hold values from -6 to 6
- values: bfloat16 [8, 4, 128, 512], P('pb', 'ka', None, 'ha'), may hold values from -6 to 6
- q_order: int32 [32], P('pb'), may hold values from 0 to 31, as said below
- block_mask: int32 [32, 32], P('pb'), may hold values from 0 to 1, as said below
Outputs:
- attended: bfloat16 [4096, 4096], P(('pb', 'ka'), 'ha')
Inputs may be any that keep to these rules, and one draw needn't show every extreme that they name: `q_order`: slots 2m and 2m+1 hold query blocks i and 31 - i for some i, in either order; every block sits in exactly one slot. block_mask[s, b] is 1 only where b <= q_order[s], and block_mask[s, q_order[s]] is 1. For every m and every r below 4, slots 2m and 2m+1 together list at most 4 key blocks b with b % 4 == r, and exactly 4 for some m and r in every draw.
All inputs are finite; a program needn't handle non-finite values.
Results may differ from a plain program's by a relative error of at most 0.0042.
Values may be sent and summed in bfloat16 or wider, within the bound.
No kernel may reach another device: no remote copies, remote signals or barrier semaphores. Data moves between devices by JAX's collectives and lax.ppermute only.
A program may use at most 128 MiB of HBM per device.

v0:
```python
import functools
import math

import jax
import jax.numpy as jnp
from jax import lax
from jax.experimental import pallas as pl
from jax.experimental.pallas import tpu as pltpu
from jax.sharding import PartitionSpec as P

HEAD_DIM = 128
MASKED = -1e30
HIDDEN = -1e38
HEADROOM = 64.0
PARTS = 8
LIMIT = 10
STAGES = 4


def folded(size):
    return list(range(0, size, 2)) + list(range(1, size, 2))[::-1]


def along_ring(array, size, step):
    ring = folded(size)
    return lax.ppermute(array, "pb", [(ring[i], ring[(i + step) % size]) for i in range(size)])


def ring_source(at, size, hops):
    place = jnp.where(at % 2 == 0, at // 2, size - 1 - at // 2)
    place = lax.rem(place + (size - hops), size)
    return jnp.where(place < (size + 1) // 2, 2 * place, 2 * (size - 1 - place) + 1)


def turn(array, size, cores, ring_step, core_step):
    rings = size // cores
    pairs = []
    for ring in range(rings):
        for core in range(cores):
            to = ((ring + ring_step) % rings) * cores + (core + core_step) % cores
            pairs.append((ring * cores + core, to))
    return lax.ppermute(array, "ka", pairs)


def dot(a, b, b_dim):
    return lax.dot_general(a, b, (((1,), (b_dim,)), ((), ())), preferred_element_type=jnp.float32)


def copy_rows(source, target, sems):
    step = source.shape[0] // PARTS
    copies = [
        pltpu.make_async_copy(
            source.at[pl.ds(i * step, step)], target.at[pl.ds(i * step, step)], sems.at[i]
        )
        for i in range(PARTS)
    ]
    for copy in copies:
        copy.start()
    return copies


def attend_stage(plan, first, last, ahead, table_ref, q_ref, *refs):
    pb, ka, cores, places, earlier, slots, turned = plan
    count = len(places)
    pieces, refs = refs[:count], refs[count:]
    old_pieces, refs = refs[:ahead], refs[ahead:]
    if not first:
        refs = refs[1:]
    acc, refs = refs[0], refs[1:]
    if last:
        out_ref, refs = refs[0], refs[1:]
    k_pool, v_pool, entries, units, refs = *refs[:4], refs[4:]
    rows = acc.shape[1]
    held, block_rows, _ = pieces[0].shape
    held = held // 2
    group = rows // block_rows
    rings = ka // cores
    own_slots = slots // cores
    p_at, k_at = lax.axis_index("pb"), lax.axis_index("ka")
    ring_at, core_at = k_at // cores, lax.rem(k_at, cores)
    scale = math.log2(math.e) / math.sqrt(HEAD_DIM)
    class_local = held // len(places[0][0])
    nothing = count * held

    def ids(where):
        found = []
        for hops, y, c in where:
            ring = lax.rem(ring_at + (rings - y), rings)
            core = lax.rem(core_at + (cores - c), cores)
            for z in hops:
                source = ring_source(p_at, pb, z)
                for t in range(class_local):
                    found.append((source * class_local + t) * ka + ring * cores + core)
        return found

    def pool_from(refs_in, at, k_out, v_out):
        for i, piece in enumerate(refs_in):
            span = slice(at + i * held, at + (i + 1) * held)
            k_out[span] = piece[:held]
            v_out[span, :, :HEAD_DIM] = piece[held:]
            v_out[span, :, HEAD_DIM:] = jnp.ones(piece[held:].shape, v_out.dtype)

    if last:
        mine = lax.rem(core_at + turned, cores) * own_slots
        slot_ids = [mine + i for i in range(own_slots)]
    else:
        slot_ids = list(range(slots))

    row_id = lax.broadcasted_iota(jnp.int32, (block_rows, block_rows), 0)
    col_id = lax.broadcasted_iota(jnp.int32, (block_rows, block_rows), 1)
    pool_from(pieces, 0, k_pool, v_pool)
    k_pool[nothing] = jnp.zeros(k_pool.shape[1:], k_pool.dtype)
    v_pool[nothing] = jnp.zeros(v_pool.shape[1:], v_pool.dtype)
    if first:
        acc[...] = jnp.zeros(acc.shape, acc.dtype)

    blocks = ids(places)
    unit_count = jnp.int32(0)
    for s in slot_ids:
        row = ring_at * slots + s
        own = table_ref[row, 0]
        place = 2 * unit_count
        for index, block in enumerate(blocks):
            entries[place] = jnp.where(block == own, index + nothing + 1, index)
            place = place + table_ref[row, 1 + block]
        entries[place] = nothing
        ends = lax.div(place + 1, 2)

        def mark(u, carry, s=s):
            units[u] = s
            return carry

        lax.fori_loop(unit_count, ends, mark, 0)
        unit_count = ends
    entries[2 * unit_count] = nothing
    entries[2 * unit_count + 1] = nothing
    units[unit_count] = slot_ids[0]

    def query_rows(s):
        return jnp.concatenate(
            [
                q_ref[
                    pl.ds(pl.multiple_of(s * block_rows, block_rows), block_rows),
                    x * HEAD_DIM : (x + 1) * HEAD_DIM,
                ]
                for x in range(group)
            ],
            axis=0,
        )

    def unit_sums(s, index, owns):
        scores = dot(query_rows(s), jnp.concatenate([k_pool[i] for i in index], axis=0), 1)
        power = scores * scale
        if owns is not None:
            reach = jnp.concatenate(
                [
                    jnp.where(col_id <= row_id + jnp.where(own, 0, block_rows), 0.0, HIDDEN)
                    for own in owns
                ],
                axis=1,
            )
            power = power + jnp.concatenate([reach] * group, axis=0)
        weights = jnp.exp2(power).astype(jnp.bfloat16)
        return dot(weights, jnp.concatenate([v_pool[i] for i in index], axis=0), 0)

    def two_units(i, carry):
        raw = [entries[4 * i + j] for j in range(4)]
        owns = [entry > nothing for entry in raw]
        index = [
            jnp.where(own, entry - (nothing + 1), entry) for own, entry in zip(owns, raw)
        ]
        which = [units[2 * i], units[2 * i + 1]]
        some = functools.reduce(jnp.logical_or, owns)

        def take(masked):
            added = [
                unit_sums(
                    which[j],
                    index[2 * j : 2 * j + 2],
                    owns[2 * j : 2 * j + 2] if masked else None,
                )
                for j in range(2)
            ]
            for j in range(2):
                acc[which[j]] += added[j]

        pl.when(some)(functools.partial(take, True))
        pl.when(jnp.logical_not(some))(functools.partial(take, False))
        return carry

    lax.fori_loop(0, lax.div(unit_count + 1, 2), two_units, 0)
    if not last:
        return

    top, k_all, v_all = refs

    def finish(s, i):
        under = acc[s, :, HEAD_DIM:]
        result = (acc[s, :, :HEAD_DIM] / under).astype(out_ref.dtype)
        for x in range(group):
            out_ref[
                i * block_rows : (i + 1) * block_rows, x * HEAD_DIM : (x + 1) * HEAD_DIM
            ] = result[x * block_rows : (x + 1) * block_rows]
        low = high = [under[j : j + 8] for j in range(0, rows, 8)]
        while len(low) > 1:
            low = [functools.reduce(jnp.minimum, low[j : j + 2]) for j in range(0, len(low), 2)]
            high = [functools.reduce(jnp.maximum, high[j : j + 2]) for j in range(0, len(high), 2)]
        return low[0], high[0]

    low, high = zip(*[finish(s, i) for i, s in enumerate(slot_ids)])
    low, high = functools.reduce(jnp.minimum, low), functools.reduce(jnp.maximum, high)
    safe = (low > 2.0**-HEADROOM) & (high < 2.0**HEADROOM)

    @pl.when(jnp.min(jnp.where(safe, 1.0, 0.0)) < 0.5)
    def _():
        pool_from(old_pieces, 0, k_all, v_all)
        pool_from(pieces, len(earlier) * held, k_all, v_all)
        blocks_all = ids(earlier) + blocks
        for i, s in enumerate(slot_ids):
            row = ring_at * slots + s
            own = table_ref[row, 0]
            place = jnp.int32(0)
            for index, block in enumerate(blocks_all):
                entries[place] = jnp.where(block == own, index + len(blocks_all), index)
                place = place + table_ref[row, 1 + block]
            acc[s] = jnp.zeros(acc.shape[1:], acc.dtype)
            top[...] = jnp.full(top.shape, MASKED, top.dtype)

            def one_block(e, carry, s=s):
                is_own = entries[e] >= len(blocks_all)
                index = jnp.where(is_own, entries[e] - len(blocks_all), entries[e])
                reach = jnp.where(
                    col_id <= row_id + jnp.where(is_own, 0, block_rows), 0.0, HIDDEN
                )
                scores = dot(query_rows(s), k_all[index], 1)
                weights, shrinks = [], []
                for x in range(group):
                    span = slice(x * block_rows, (x + 1) * block_rows)
                    power = scores[span] * scale + reach
                    new = jnp.maximum(top[span], jnp.max(power, axis=1, keepdims=True))
                    shrink = jnp.exp2(top[span] - new)
                    top[span] = new
                    weights.append(jnp.exp2(power - new).astype(jnp.bfloat16))
                    shrinks.append(jnp.concatenate([shrink, shrink], axis=1))
                added = dot(jnp.concatenate(weights, axis=0), v_all[index], 0)
                acc[s] = acc[s] * jnp.concatenate(shrinks, axis=0) + added
                return carry

            lax.fori_loop(0, place, one_block, 0)
            finish(s, i)


def split(cores, keys_ref, values_ref, *refs):
    outs, sems = refs[:cores], refs[cores]
    count = keys_ref.shape[0]
    width = outs[0].shape[2]
    core = lax.rem(lax.axis_index("ka"), cores)
    copies = []
    for i, out in enumerate(outs):
        column = pl.multiple_of(lax.rem(core + i, cores) * width, HEAD_DIM)
        for j, ref in enumerate((keys_ref, values_ref)):
            copy = pltpu.make_async_copy(
                ref.at[:, 0, :, pl.ds(column, width)],
                out.at[pl.ds(j * count, count)],
                sems.at[2 * i + j],
            )
            copy.start()
            copies.append(copy)
    for copy in copies:
        copy.wait()


def fetch(cores, queries_ref, out_ref, sems):
    rows, width = out_ref.shape
    at = lax.axis_index("ka")
    copies = copy_rows(
        queries_ref.at[
            pl.ds(pl.multiple_of(at // cores * rows, HEAD_DIM), rows),
            pl.ds(pl.multiple_of(lax.rem(at, cores) * width, HEAD_DIM), width),
        ],
        out_ref,
        sems,
    )
    for copy in copies:
        copy.wait()


def join(cores, own_ref, other_ref, out_ref, sems):
    width = own_ref.shape[1]
    core = lax.rem(lax.axis_index("ka"), cores)
    copies = []
    for i, ref in enumerate((own_ref, other_ref)):
        at = pl.multiple_of(lax.rem(core + (cores - i), cores) * width, HEAD_DIM)
        copies += copy_rows(ref, out_ref.at[:, pl.ds(at, width)], sems.at[i])
    for copy in copies:
        copy.wait()


def on_device(queries, keys, values, q_order, block_mask):
    pb, ka = lax.axis_size("pb"), lax.axis_size("ka")
    class_local, _, block_rows, kv_width = keys.shape
    cores = 2 if ka % 2 == 0 and kv_width == 2 * HEAD_DIM else 1
    rings = ka // cores
    head_width = kv_width // cores
    width = queries.shape[1] // cores
    rows = width // head_width * block_rows
    own_slots = queries.shape[0] // block_rows // ka
    slots = own_slots * cores

    vmem = pl.BlockSpec(memory_space=pltpu.VMEM)
    smem = pl.BlockSpec(memory_space=pltpu.SMEM)
    hbm = pl.BlockSpec(memory_space=pltpu.HBM)
    anywhere = pl.BlockSpec(memory_space=pl.ANY)
    stages = min(STAGES, pb)
    sources = pb // stages

    table = jnp.concatenate([q_order[:, None], block_mask], axis=1)
    part = jax.ShapeDtypeStruct((2 * class_local, block_rows, head_width), keys.dtype)
    starts = pl.pallas_call(
        functools.partial(split, cores),
        out_shape=[part] * cores,
        in_specs=[anywhere] * 2,
        out_specs=[vmem] * cores,
        scratch_shapes=[pltpu.SemaphoreType.DMA((2 * cores,))],
        compiler_params=pltpu.CompilerParams(vmem_limit_bytes=54 * 2**20),
    )(keys, values)
    own_queries = pl.pallas_call(
        functools.partial(fetch, cores),
        out_shape=jax.ShapeDtypeStruct((slots * block_rows, width), queries.dtype),
        in_specs=[anywhere],
        out_specs=vmem,
        scratch_shapes=[pltpu.SemaphoreType.DMA((PARTS,))],
        compiler_params=pltpu.CompilerParams(vmem_limit_bytes=50 * 2**20),
    )(queries)
    if cores == 2:
        starts = [starts[0], turn(starts[1], ka, cores, 0, 1)]

    near = {0: starts}
    order = [0]
    for hop in range(1, pb // 2 + 1):
        for z, step in ((hop, 1), (pb - hop, -1)):
            if z not in near:
                near[z] = [along_ring(array, pb, step) for array in near[(z - step) % pb]]
                order.append(z)
    staged = []
    for stage in range(stages):
        here = [near[z] for z in order[stage * sources : (stage + 1) * sources]]
        if sources == 1:
            staged.append(here[0])
            continue
        staged.append(
            [
                jnp.concatenate(
                    [array[:class_local] for array in arrays]
                    + [array[class_local:] for array in arrays],
                    axis=0,
                )
                for arrays in zip(*here)
            ]
        )

    def call(first, last, turned, pieces, places, earlier, own_queries, state, extra):
        held = len(places) * sources * class_local
        everything = held + len(earlier) * sources * class_local
        here = own_slots if last else slots
        outs = [jax.ShapeDtypeStruct((slots, rows, 2 * HEAD_DIM), jnp.float32)]
        scratch = [
            pltpu.VMEM((held + 1, block_rows, HEAD_DIM), jnp.bfloat16),
            pltpu.VMEM((held + 1, block_rows, 2 * HEAD_DIM), jnp.bfloat16),
            pltpu.SMEM((max(here * (held + 1) + 2, everything + 1),), jnp.int32),
            pltpu.SMEM((here * (held // 2 + 1) + 1,), jnp.int32),
        ]
        if last:
            outs.append(jax.ShapeDtypeStruct((own_slots * block_rows, width), queries.dtype))
            scratch += [
                pltpu.VMEM((rows, HEAD_DIM), jnp.float32),
                pltpu.VMEM((everything, block_rows, HEAD_DIM), jnp.bfloat16),
                pltpu.VMEM((everything, block_rows, 2 * HEAD_DIM), jnp.bfloat16),
            ]
        pooled = held + (everything if last else 0)
        room = LIMIT * 2**20 + pooled * block_rows * HEAD_DIM * 6
        state_at = 2 + len(places) + len(extra)
        return pl.pallas_call(
            functools.partial(
                attend_stage,
                (pb, ka, cores, places, earlier, slots, turned),
                first,
                last,
                len(extra),
            ),
            out_shape=outs,
            in_specs=[smem]
            + [vmem] * (1 + len(places))
            + [vmem if last else anywhere] * len(extra)
            + [vmem] * len(state),
            out_specs=[vmem] * len(outs),
            input_output_aliases={state_at + i: i for i in range(len(state))},
            scratch_shapes=scratch,
            compiler_params=pltpu.CompilerParams(vmem_limit_bytes=room),
            cost_estimate=pl.CostEstimate(
                flops=2**31, bytes_accessed=2**22, transcendentals=2**20
            ),
        )(table, own_queries, *pieces, *extra, *state)

    placed = []
    for stage in range(stages):
        hops = order[stage * sources : (stage + 1) * sources]
        places, pieces = [], []
        for c in range(cores):
            ring = staged[stage][c]
            for y in range(rings):
                if y:
                    ring = turn(ring, ka, cores, 1, 0)
                places.append((hops, y, c))
                pieces.append(ring)
        placed.append((places, pieces))
    state, earlier, before = [], [], []
    for stage in range(stages - 1):
        places, pieces = placed[stage]
        ahead = [staged[stage + 1][-1]]
        state = call(stage == 0, False, 0, pieces, places, earlier, own_queries, state, ahead)
        earlier, before = earlier + places, before + pieces
    places, pieces = placed[-1]
    halves = []
    for c in reversed(range(cores)):
        *state, half = call(False, True, c, pieces, places, earlier, own_queries, state, before)
        halves.append(half)
    if cores == 1:
        return halves[0]
    return pl.pallas_call(
        functools.partial(join, cores),
        out_shape=jax.ShapeDtypeStruct((own_slots * block_rows, cores * width), queries.dtype),
        in_specs=[vmem] * 2,
        out_specs=anywhere,
        scratch_shapes=[pltpu.SemaphoreType.DMA((cores, PARTS))],
    )(halves[1], turn(halves[0], ka, cores, 0, 1))


def solution(mesh):
    in_specs = (
        P("pb", "ha"),
        P("pb", "ka", None, "ha"),
        P("pb", "ka", None, "ha"),
        P("pb"),
        P("pb", None),
    )
    out_specs = P(("pb", "ka"), "ha")
    return jax.shard_map(
        on_device, mesh=mesh, in_specs=in_specs, out_specs=out_specs, check_vma=False
    )
```

profile of v0, /device:TPU:9, one launch (start us, length us, event | category | flops | bytes accessed | tf_op | source)
XLA Modules:
  0.0 66.6 jit_solution(3891968833825696575)
XLA Ops:
  0.0 1.7 %shard_map.56 = (bf16[4,128,128]{2,1,0:T(8,128)(2,1)}, bf16[4,128,128]{2,1,0:T(8,128)(2,1)}) custom-call(bf16[2,1,128,256]{3,2,1,0:T(8,128)(2,1)} %keys_ref.1, bf16[2,1,128,256]{3,2,1,0:T(8,128)(2,1)} %values_ref.1), custom_call_target="tpu_custom_call" | custom-call | tf_op jit(solution)/shard_map/pallas_call | solution.py:319
  1.7 0.0 copy-start.1
  1.7 0.7 %collective-permute-start.3 = (bf16[4,128,128]{2,1,0:T(8,128)(2,1)}, bf16[4,128,128]{2,1,0:T(8,128)(2,1)S(1)}, u32[]{:S(2)}, u32[]{:S(2)}) collective-permute-start(bf16[4,128,128]{2,1,0:T(8,128)(2,1)} %get-tuple-element.11), channel_id=1, source_target_pairs={{0,2},{2,0},{4,6},{6,4},{1,3},{3,1},{5,7},{7,5},{8,10},{10,8},{12,... | collective-permute-start | bytes 393224 | tf_op jit(solution)/shard_map/ppermute | solution.py:42
  2.4 2.3 %collective-permute-start.11 = (bf16[4,128,128]{2,1,0:T(8,128)(2,1)}, bf16[4,128,128]{2,1,0:T(8,128)(2,1)S(1)}, u32[]{:S(2)}, u32[]{:S(2)}) collective-permute-start(bf16[4,128,128]{2,1,0:T(8,128)(2,1)} %get-tuple-element.10.refs_0_.refs_4_), channel_id=1, source_target_pairs={{0,8},{16,0},{24,16},{8,24},{1,9},{17,1},{25,17},{9,25},{2,10},{18... | collective-permute-start | bytes 393224 | tf_op jit(solution)/shard_map/ppermute | solution.py:26
  4.7 0.0 collective-permute-start
  4.7 1.2 %collective-permute-start.7 = (bf16[4,128,128]{2,1,0:T(8,128)(2,1)}, bf16[4,128,128]{2,1,0:T(8,128)(2,1)S(1)}, u32[]{:S(2)}, u32[]{:S(2)}) collective-permute-start(bf16[4,128,128]{2,1,0:T(8,128)(2,1)} %get-tuple-element.10.refs_0_.refs_4_), channel_id=1, source_target_pairs={{0,4},{2,6},{4,0},{6,2},{1,5},{3,7},{5,1},{7,3},{8,12},{10,14},{12... | collective-permute-start | bytes 393224 | tf_op jit(solution)/shard_map/ppermute | solution.py:42
  6.0 0.0 collective-permute-done.3.refs_2_.refs_6_
  6.0 0.2 collective-permute-start.4
  6.2 0.2 collective-permute-start.8
  6.4 0.7 %copy.10 = s32[8,1]{1,0:T(8,128)S(1)} copy(s32[8,1]{0,1:T(1,128)} %bitcast.1) | data formatting | bytes 64 | tf_op jit(solution)/shard_map/broadcast_in_dim | solution.py:317
  7.1 1.3 %shard_map.55.q_ref = bf16[512,1024]{1,0:T(8,128)(2,1)S(1)} custom-call(bf16[1024,2048]{1,0:T(8,128)(2,1)} %queries_ref.1), custom_call_target="tpu_custom_call" | custom-call | tf_op jit(solution)/shard_map/pallas_call | solution.py:327
  8.5 0.0 copy-done.3
  8.5 0.1 pad_add_fusion.table_ref
  8.6 4.9 %collective-permute-done.11.refs_0_.refs_12_ = bf16[4,128,128]{2,1,0:T(8,128)(2,1)S(1)} collective-permute-done((bf16[4,128,128]{2,1,0:T(8,128)(2,1)}, bf16[4,128,128]{2,1,0:T(8,128)(2,1)S(1)}, u32[]{:S(2)}, u32[]{:S(2)}) %collective-permute-start.11) | collective-permute-done | bytes 131104 | tf_op jit(solution)/shard_map/ppermute | solution.py:26
  13.4 3.1 %collective-permute-start.13 = (bf16[4,128,128]{2,1,0:T(8,128)(2,1)S(1)}, bf16[4,128,128]{2,1,0:T(8,128)(2,1)S(1)}, u32[]{:S(2)}, u32[]{:S(2)}) collective-permute-start(bf16[4,128,128]{2,1,0:T(8,128)(2,1)S(1)} %collective-permute-done.3.refs_2_.refs_6_), channel_id=1, source_target_pairs={{0,8},{16,0},{24,16},{8,24},{1,9},{17,1},{25,17},{9,25},{2,10},{18... | collective-permute-start | bytes 393224 | tf_op jit(solution)/shard_map/ppermute | solution.py:26
  16.6 0.0 collective-permute-done.refs_0_.refs_8_
  16.6 1.2 %collective-permute-start.9 = (bf16[4,128,128]{2,1,0:T(8,128)(2,1)S(1)}, bf16[4,128,128]{2,1,0:T(8,128)(2,1)S(1)}, u32[]{:S(2)}, u32[]{:S(2)}) collective-permute-start(bf16[4,128,128]{2,1,0:T(8,128)(2,1)S(1)} %collective-permute-done.refs_0_.refs_8_), channel_id=1, source_target_pairs={{0,4},{2,6},{4,0},{6,2},{1,5},{3,7},{5,1},{7,3},{8,12},{10,14},{12... | collective-permute-start | bytes 393224 | tf_op jit(solution)/shard_map/ppermute | solution.py:42
  17.8 0.0 collective-permute-done.7.refs_1_.refs_5_
  17.8 0.0 collective-permute-start.1
  17.8 0.0 collective-permute-done.4.refs_4_.refs_2_.refs_10_
  17.8 0.3 collective-permute-start.10
  18.1 0.0 collective-permute-done.8.refs_3_.refs_7_
  18.1 0.0 collective-permute-start.5
  18.1 0.0 copy-done.1
  18.1 2.8 %shard_map.57.refs_5_ = f32[4,1024,256]{2,1,0:T(8,128)S(1)} custom-call(s32[8,33]{1,0:T(8,128)S(1)} %pad_add_fusion.table_ref, bf16[512,1024]{1,0:T(8,128)(2,1)S(1)} %shard_map.55.q_ref, bf16[4,128,128]{2,1,0:T(8,128)(2,1)S(1)} %copy-done.1, bf16[4,128,128]{2,1,0:T(8,128)(2,1)S(1)} %collective-permute-done.7.refs_1_.refs_5_, ...), custom_call_target="tpu_custom_call" | custom-call | flops 2147483648 | bytes 4194304 | tf_op jit(solution)/shard_map/pallas_call | solution.py:383
  20.9 3.5 %collective-permute-done.13.refs_4_.refs_2_.refs_14_ = bf16[4,128,128]{2,1,0:T(8,128)(2,1)S(1)} collective-permute-done((bf16[4,128,128]{2,1,0:T(8,128)(2,1)S(1)}, bf16[4,128,128]{2,1,0:T(8,128)(2,1)S(1)}, u32[]{:S(2)}, u32[]{:S(2)}) %collective-permute-start.13) | collective-permute-done | bytes 131104 | tf_op jit(solution)/shard_map/ppermute | solution.py:26
  24.5 1.2 %collective-permute-start.12 = (bf16[4,128,128]{2,1,0:T(8,128)(2,1)S(1)}, bf16[4,128,128]{2,1,0:T(8,128)(2,1)S(1)}, u32[]{:S(2)}, u32[]{:S(2)}) collective-permute-start(bf16[4,128,128]{2,1,0:T(8,128)(2,1)S(1)} %collective-permute-done.11.refs_0_.refs_12_), channel_id=1, source_target_pairs={{0,4},{2,6},{4,0},{6,2},{1,5},{3,7},{5,1},{7,3},{8,12},{10,14},{12... | collective-permute-start | bytes 393224 | tf_op jit(solution)/shard_map/ppermute | solution.py:42
  25.7 0.0 collective-permute-done.9.refs_1_.refs_9_
  25.7 0.2 collective-permute-start.14
  26.0 0.0 collective-permute-done.1.refs_0_
  26.0 1.2 %collective-permute-start.2 = (bf16[4,128,128]{2,1,0:T(8,128)(2,1)S(1)}, bf16[4,128,128]{2,1,0:T(8,128)(2,1)S(1)}, u32[]{:S(2)}, u32[]{:S(2)}) collective-permute-start(bf16[4,128,128]{2,1,0:T(8,128)(2,1)S(1)} %collective-permute-done.1.refs_0_), channel_id=1, source_target_pairs={{0,4},{2,6},{4,0},{6,2},{1,5},{3,7},{5,1},{7,3},{8,12},{10,14},{12... | collective-permute-start | bytes 393224 | tf_op jit(solution)/shard_map/ppermute | solution.py:42
  27.2 0.0 collective-permute-done.5.refs_4_.refs_2_
  27.2 0.2 collective-permute-start.6
  27.4 0.0 collective-permute-done.10.refs_3_.refs_11_
  27.4 1.7 %shard_map.58.refs_5_ = f32[4,1024,256]{2,1,0:T(8,128)S(1)} custom-call(s32[8,33]{1,0:T(8,128)S(1)} %pad_add_fusion.table_ref, bf16[512,1024]{1,0:T(8,128)(2,1)S(1)} %shard_map.55.q_ref, bf16[4,128,128]{2,1,0:T(8,128)(2,1)S(1)} %collective-permute-done.refs_0_.refs_8_, ...), custom_call_target="tpu_custom_call", output_to_operand_aliasing={{}: (7, {})} | custom-call | flops 2147483648 | bytes 4194304 | tf_op jit(solution)/shard_map/pallas_call | solution.py:383
  29.1 0.0 collective-permute-done.12.refs_1_.refs_13_
  29.1 2.0 %collective-permute-done.14.refs_3_.refs_15_ = bf16[4,128,128]{2,1,0:T(8,128)(2,1)S(1)} collective-permute-done((bf16[4,128,128]{2,1,0:T(8,128)(2,1)S(1)}, bf16[4,128,128]{2,1,0:T(8,128)(2,1)S(1)}, u32[]{:S(2)}, u32[]{:S(2)}) %collective-permute-start.14) | collective-permute-done | bytes 131104 | tf_op jit(solution)/shard_map/ppermute | solution.py:42
  31.2 3.4 %shard_map.59.refs_16_ = f32[4,1024,256]{2,1,0:T(8,128)S(1)} custom-call(s32[8,33]{1,0:T(8,128)S(1)} %pad_add_fusion.table_ref, bf16[512,1024]{1,0:T(8,128)(2,1)S(1)} %shard_map.55.q_ref, bf16[4,128,128]{2,1,0:T(8,128)(2,1)S(1)} %collective-permute-done.11.refs_0_.refs_12_, ...), custom_call_target="tpu_custom_call", output_to_operand_aliasing={{}: (7, {})} | custom-call | flops 2147483648 | bytes 4194304 | tf_op jit(solution)/shard_map/pallas_call | solution.py:383
  34.5 0.0 collective-permute-done.2.refs_1_
  34.5 2.2 %collective-permute-done.6.refs_3_ = bf16[4,128,128]{2,1,0:T(8,128)(2,1)S(1)} collective-permute-done((bf16[4,128,128]{2,1,0:T(8,128)(2,1)S(1)}, bf16[4,128,128]{2,1,0:T(8,128)(2,1)S(1)}, u32[]{:S(2)}, u32[]{:S(2)}) %collective-permute-start.6) | collective-permute-done | bytes 131104 | tf_op jit(solution)/shard_map/ppermute | solution.py:42
  36.8 2.1 %shard_map.60 = (f32[4,1024,256]{2,1,0:T(8,128)S(1)}, bf16[256,1024]{1,0:T(8,128)(2,1)S(1)}) custom-call(s32[8,33]{1,0:T(8,128)S(1)} %pad_add_fusion.table_ref, bf16[512,1024]{1,0:T(8,128)(2,1)S(1)} %shard_map.55.q_ref, bf16[4,128,128]{2,1,0:T(8,128)(2,1)S(1)} %collective-permute-done.1.refs_0_, ...), custom_call_target="tpu_custom_call", output_to_operand_aliasing={{0}: (18, {})} | custom-call | flops 2147483648 | bytes 4194304 | tf_op jit(solution)/shard_map/pallas_call | solution.py:383
  38.8 11.8 %collective-permute-start.15 = (bf16[256,1024]{1,0:T(8,128)(2,1)S(1)}, bf16[256,1024]{1,0:T(8,128)(2,1)S(1)}, u32[]{:S(2)}, u32[]{:S(2)}) collective-permute-start(bf16[256,1024]{1,0:T(8,128)(2,1)S(1)} %get-tuple-element.14), channel_id=1, source_target_pairs={{0,2},{2,0},{4,6},{6,4},{1,3},{3,1},{5,7},{7,5},{8,10},{10,8},{12,... | collective-permute-start | bytes 1572872 | tf_op jit(solution)/shard_map/ppermute | solution.py:42
  50.6 11.9 %shard_map.61 = (f32[4,1024,256]{2,1,0:T(8,128)S(1)}, bf16[256,1024]{1,0:T(8,128)(2,1)S(1)}) custom-call(s32[8,33]{1,0:T(8,128)S(1)} %pad_add_fusion.table_ref, bf16[512,1024]{1,0:T(8,128)(2,1)S(1)} %shard_map.55.q_ref, bf16[4,128,128]{2,1,0:T(8,128)(2,1)S(1)} %collective-permute-done.1.refs_0_, ...), custom_call_target="tpu_custom_call", output_to_operand_aliasing={{0}: (18, {})} | custom-call | flops 2147483648 | bytes 4194304 | tf_op jit(solution)/shard_map/pallas_call | solution.py:383
  62.6 0.0 copy-start
  62.6 0.8 %copy-done = bf16[256,1024]{1,0:T(8,128)(2,1)} copy-done((bf16[256,1024]{1,0:T(8,128)(2,1)}, bf16[256,1024]{1,0:T(8,128)(2,1)S(1)}, u32[]{:S(2)}) %copy-start) | copy-done | bytes 524312
  63.4 0.0 collective-permute-done.15.other_ref
  63.4 0.8 %copy-done.2 = bf16[256,1024]{1,0:T(8,128)(2,1)} copy-done((bf16[256,1024]{1,0:T(8,128)(2,1)}, bf16[256,1024]{1,0:T(8,128)(2,1)S(1)}, u32[]{:S(2)}) %copy-start.2) | copy-done | bytes 524312
  64.2 2.3 %shard_map.62 = bf16[256,2048]{1,0:T(8,128)(2,1)} custom-call(bf16[256,1024]{1,0:T(8,128)(2,1)} %copy-done, bf16[256,1024]{1,0:T(8,128)(2,1)} %copy-done.2), custom_call_target="tpu_custom_call" | custom-call | tf_op jit(solution)/shard_map/pallas_call | solution.py:430
  (2 shorter events, 0.0 us)
Async XLA Ops:
  0.0 8.5 %copy-start.3 = (s32[8,32]{1,0:T(8,128)S(1)}, s32[8,32]{1,0:T(8,128)}, u32[]{:S(2)}) copy-start(s32[8,32]{1,0:T(8,128)} %param.9) | copy-start | bytes 3076
  1.7 16.5 %copy-start.1 = (bf16[4,128,128]{2,1,0:T(8,128)(2,1)S(1)}, bf16[4,128,128]{2,1,0:T(8,128)(2,1)}, u32[]{:S(2)}) copy-start(bf16[4,128,128]{2,1,0:T(8,128)(2,1)} %get-tuple-element.10.refs_0_.refs_4_) | copy-start | bytes 393220
  1.7 4.3 %collective-permute-start.3 = (bf16[4,128,128]{2,1,0:T(8,128)(2,1)}, bf16[4,128,128]{2,1,0:T(8,128)(2,1)S(1)}, u32[]{:S(2)}, u32[]{:S(2)}) collective-permute-start(bf16[4,128,128]{2,1,0:T(8,128)(2,1)} %get-tuple-element.11), channel_id=1, source_target_pairs={{0,2},{2,0},{4,6},{6,4},{1,3},{3,1},{5,7},{7,5},{8,10},{10,8},{12,... | collective-permute-start | bytes 393224 | tf_op jit(solution)/shard_map/ppermute | solution.py:42
  2.4 11.0 %collective-permute-start.11 = (bf16[4,128,128]{2,1,0:T(8,128)(2,1)}, bf16[4,128,128]{2,1,0:T(8,128)(2,1)S(1)}, u32[]{:S(2)}, u32[]{:S(2)}) collective-permute-start(bf16[4,128,128]{2,1,0:T(8,128)(2,1)} %get-tuple-element.10.refs_0_.refs_4_), channel_id=1, source_target_pairs={{0,8},{16,0},{24,16},{8,24},{1,9},{17,1},{25,17},{9,25},{2,10},{18... | collective-permute-start | bytes 393224 | tf_op jit(solution)/shard_map/ppermute | solution.py:26
  4.7 11.8 %collective-permute-start = (bf16[4,128,128]{2,1,0:T(8,128)(2,1)}, bf16[4,128,128]{2,1,0:T(8,128)(2,1)S(1)}, u32[]{:S(2)}, u32[]{:S(2)}) collective-permute-start(bf16[4,128,128]{2,1,0:T(8,128)(2,1)} %get-tuple-element.10.refs_0_.refs_4_), channel_id=1, source_target_pairs={{0,16},{16,24},{24,8},{8,0},{1,17},{17,25},{25,9},{9,1},{2,18},{18... | collective-permute-start | bytes 393224 | tf_op jit(solution)/shard_map/ppermute | solution.py:26
  4.7 13.1 %collective-permute-start.7 = (bf16[4,128,128]{2,1,0:T(8,128)(2,1)}, bf16[4,128,128]{2,1,0:T(8,128)(2,1)S(1)}, u32[]{:S(2)}, u32[]{:S(2)}) collective-permute-start(bf16[4,128,128]{2,1,0:T(8,128)(2,1)} %get-tuple-element.10.refs_0_.refs_4_), channel_id=1, source_target_pairs={{0,4},{2,6},{4,0},{6,2},{1,5},{3,7},{5,1},{7,3},{8,12},{10,14},{12... | collective-permute-start | bytes 393224 | tf_op jit(solution)/shard_map/ppermute | solution.py:42
  6.0 11.8 %collective-permute-start.4 = (bf16[4,128,128]{2,1,0:T(8,128)(2,1)S(1)}, bf16[4,128,128]{2,1,0:T(8,128)(2,1)S(1)}, u32[]{:S(2)}, u32[]{:S(2)}) collective-permute-start(bf16[4,128,128]{2,1,0:T(8,128)(2,1)S(1)} %collective-permute-done.3.refs_2_.refs_6_), channel_id=1, source_target_pairs={{0,16},{16,24},{24,8},{8,0},{1,17},{17,25},{25,9},{9,1},{2,18},{18... | collective-permute-start | bytes 393224 | tf_op jit(solution)/shard_map/ppermute | solution.py:26
  6.2 11.9 %collective-permute-start.8 = (bf16[4,128,128]{2,1,0:T(8,128)(2,1)S(1)}, bf16[4,128,128]{2,1,0:T(8,128)(2,1)S(1)}, u32[]{:S(2)}, u32[]{:S(2)}) collective-permute-start(bf16[4,128,128]{2,1,0:T(8,128)(2,1)S(1)} %collective-permute-done.3.refs_2_.refs_6_), channel_id=1, source_target_pairs={{0,4},{2,6},{4,0},{6,2},{1,5},{3,7},{5,1},{7,3},{8,12},{10,14},{12... | collective-permute-start | bytes 393224 | tf_op jit(solution)/shard_map/ppermute | solution.py:42
  13.4 11.0 %collective-permute-start.13 = (bf16[4,128,128]{2,1,0:T(8,128)(2,1)S(1)}, bf16[4,128,128]{2,1,0:T(8,128)(2,1)S(1)}, u32[]{:S(2)}, u32[]{:S(2)}) collective-permute-start(bf16[4,128,128]{2,1,0:T(8,128)(2,1)S(1)} %collective-permute-done.3.refs_2_.refs_6_), channel_id=1, source_target_pairs={{0,8},{16,0},{24,16},{8,24},{1,9},{17,1},{25,17},{9,25},{2,10},{18... | collective-permute-start | bytes 393224 | tf_op jit(solution)/shard_map/ppermute | solution.py:26
  16.6 9.1 %collective-permute-start.9 = (bf16[4,128,128]{2,1,0:T(8,128)(2,1)S(1)}, bf16[4,128,128]{2,1,0:T(8,128)(2,1)S(1)}, u32[]{:S(2)}, u32[]{:S(2)}) collective-permute-start(bf16[4,128,128]{2,1,0:T(8,128)(2,1)S(1)} %collective-permute-done.refs_0_.refs_8_), channel_id=1, source_target_pairs={{0,4},{2,6},{4,0},{6,2},{1,5},{3,7},{5,1},{7,3},{8,12},{10,14},{12... | collective-permute-start | bytes 393224 | tf_op jit(solution)/shard_map/ppermute | solution.py:42
  17.8 8.1 %collective-permute-start.1 = (bf16[4,128,128]{2,1,0:T(8,128)(2,1)S(1)}, bf16[4,128,128]{2,1,0:T(8,128)(2,1)S(1)}, u32[]{:S(2)}, u32[]{:S(2)}) collective-permute-start(bf16[4,128,128]{2,1,0:T(8,128)(2,1)S(1)} %collective-permute-done.refs_0_.refs_8_), channel_id=1, source_target_pairs={{0,16},{16,24},{24,8},{8,0},{1,17},{17,25},{25,9},{9,1},{2,18},{18... | collective-permute-start | bytes 393224 | tf_op jit(solution)/shard_map/ppermute | solution.py:26
  17.8 9.6 %collective-permute-start.10 = (bf16[4,128,128]{2,1,0:T(8,128)(2,1)S(1)}, bf16[4,128,128]{2,1,0:T(8,128)(2,1)S(1)}, u32[]{:S(2)}, u32[]{:S(2)}) collective-permute-start(bf16[4,128,128]{2,1,0:T(8,128)(2,1)S(1)} %collective-permute-done.4.refs_4_.refs_2_.refs_10_), channel_id=1, source_target_pairs={{0,4},{2,6},{4,0},{6,2},{1,5},{3,7},{5,1},{7,3},{8,12},{10,14},{12... | collective-permute-start | bytes 393224 | tf_op jit(solution)/shard_map/ppermute | solution.py:42
  18.1 9.1 %collective-permute-start.5 = (bf16[4,128,128]{2,1,0:T(8,128)(2,1)S(1)}, bf16[4,128,128]{2,1,0:T(8,128)(2,1)S(1)}, u32[]{:S(2)}, u32[]{:S(2)}) collective-permute-start(bf16[4,128,128]{2,1,0:T(8,128)(2,1)S(1)} %collective-permute-done.4.refs_4_.refs_2_.refs_10_), channel_id=1, source_target_pairs={{0,16},{16,24},{24,8},{8,0},{1,17},{17,25},{25,9},{9,1},{2,18},{18... | collective-permute-start | bytes 393224 | tf_op jit(solution)/shard_map/ppermute | solution.py:26
  24.5 4.6 %collective-permute-start.12 = (bf16[4,128,128]{2,1,0:T(8,128)(2,1)S(1)}, bf16[4,128,128]{2,1,0:T(8,128)(2,1)S(1)}, u32[]{:S(2)}, u32[]{:S(2)}) collective-permute-start(bf16[4,128,128]{2,1,0:T(8,128)(2,1)S(1)} %collective-permute-done.11.refs_0_.refs_12_), channel_id=1, source_target_pairs={{0,4},{2,6},{4,0},{6,2},{1,5},{3,7},{5,1},{7,3},{8,12},{10,14},{12... | collective-permute-start | bytes 393224 | tf_op jit(solution)/shard_map/ppermute | solution.py:42
  25.7 5.4 %collective-permute-start.14 = (bf16[4,128,128]{2,1,0:T(8,128)(2,1)S(1)}, bf16[4,128,128]{2,1,0:T(8,128)(2,1)S(1)}, u32[]{:S(2)}, u32[]{:S(2)}) collective-permute-start(bf16[4,128,128]{2,1,0:T(8,128)(2,1)S(1)} %collective-permute-done.13.refs_4_.refs_2_.refs_14_), channel_id=1, source_target_pairs={{0,4},{2,6},{4,0},{6,2},{1,5},{3,7},{5,1},{7,3},{8,12},{10,14},{12... | collective-permute-start | bytes 393224 | tf_op jit(solution)/shard_map/ppermute | solution.py:42
  26.0 8.6 %collective-permute-start.2 = (bf16[4,128,128]{2,1,0:T(8,128)(2,1)S(1)}, bf16[4,128,128]{2,1,0:T(8,128)(2,1)S(1)}, u32[]{:S(2)}, u32[]{:S(2)}) collective-permute-start(bf16[4,128,128]{2,1,0:T(8,128)(2,1)S(1)} %collective-permute-done.1.refs_0_), channel_id=1, source_target_pairs={{0,4},{2,6},{4,0},{6,2},{1,5},{3,7},{5,1},{7,3},{8,12},{10,14},{12... | collective-permute-start | bytes 393224 | tf_op jit(solution)/shard_map/ppermute | solution.py:42
  27.2 9.6 %collective-permute-start.6 = (bf16[4,128,128]{2,1,0:T(8,128)(2,1)S(1)}, bf16[4,128,128]{2,1,0:T(8,128)(2,1)S(1)}, u32[]{:S(2)}, u32[]{:S(2)}) collective-permute-start(bf16[4,128,128]{2,1,0:T(8,128)(2,1)S(1)} %collective-permute-done.5.refs_4_.refs_2_), channel_id=1, source_target_pairs={{0,4},{2,6},{4,0},{6,2},{1,5},{3,7},{5,1},{7,3},{8,12},{10,14},{12... | collective-permute-start | bytes 393224 | tf_op jit(solution)/shard_map/ppermute | solution.py:42
  38.8 24.5 %collective-permute-start.15 = (bf16[256,1024]{1,0:T(8,128)(2,1)S(1)}, bf16[256,1024]{1,0:T(8,128)(2,1)S(1)}, u32[]{:S(2)}, u32[]{:S(2)}) collective-permute-start(bf16[256,1024]{1,0:T(8,128)(2,1)S(1)} %get-tuple-element.14), channel_id=1, source_target_pairs={{0,2},{2,0},{4,6},{6,4},{1,3},{3,1},{5,7},{7,5},{8,10},{10,8},{12,... | collective-permute-start | bytes 1572872 | tf_op jit(solution)/shard_map/ppermute | solution.py:42
  62.6 0.8 %copy-start = (bf16[256,1024]{1,0:T(8,128)(2,1)}, bf16[256,1024]{1,0:T(8,128)(2,1)S(1)}, u32[]{:S(2)}) copy-start(bf16[256,1024]{1,0:T(8,128)(2,1)S(1)} %get-tuple-element.13.own_ref) | copy-start | bytes 1572868
  63.4 0.8 %copy-start.2 = (bf16[256,1024]{1,0:T(8,128)(2,1)}, bf16[256,1024]{1,0:T(8,128)(2,1)S(1)}, u32[]{:S(2)}) copy-start(bf16[256,1024]{1,0:T(8,128)(2,1)S(1)} %collective-permute-done.15.other_ref) | copy-start | bytes 1572868
where the time goes:
time: 66.5 us; the launch traced here: 66.6 us
  Pallas kernels  27.2 us (41%)
  starting transfers between devices  24.1 us (36%)
  waiting for transfers between devices  12.7 us (19%)
  local copies, waits for them, and re-layouts  2.34 us (4%)
    pallas_call x5, Pallas kernels, call(): pl.pallas_call(functools.partial(attend_stage, (pb, ka, cores, places, ea...  21.8 us
    ppermute x10, starting transfers between devices, turn(): return lax.ppermute(array, 'ka', pairs)  18.4 us
    ppermute x6, waiting for transfers between devices, along_ring(): lax.ppermute(array, 'pb', [(ring[i], ring[(i + step) % size]) for i in ra...  8.43 us
    ppermute x6, starting transfers between devices, along_ring(): lax.ppermute(array, 'pb', [(ring[i], ring[(i + step) % size]) for i in ra...  5.68 us
    ppermute x10, waiting for transfers between devices, turn(): return lax.ppermute(array, 'ka', pairs)  4.25 us
    pallas_call x1, Pallas kernels, on_device(): pl.pallas_call(functools.partial(join, cores), out_shape=jax.ShapeDtypeSt...  2.29 us
    pallas_call x1, Pallas kernels, on_device(): pl.pallas_call(functools.partial(split, cores), out_shape=[part] * cores,...  1.67 us
    unnamed x8, local copies, waits for them, and re-layouts  1.61 us
  transfers between devices with their start and end apart: 16, of which 4 were waited for; matrix products, arithmetic and copies ran while one was open for 1% of the time, Pallas kernels for 32%

commit v1 on v0

--- a/solution.py
+++ b/solution.py
@@ -14,6 +14,7 @@
 HEADROOM = 64.0
 PARTS = 8
 LIMIT = 10
+SMALL = 4
 STAGES = 4
 
 
@@ -21,9 +22,9 @@
     return list(range(0, size, 2)) + list(range(1, size, 2))[::-1]
 
 
-def along_ring(array, size, step):
+def along_ring(array, size):
     ring = folded(size)
-    return lax.ppermute(array, "pb", [(ring[i], ring[(i + step) % size]) for i in range(size)])
+    return lax.ppermute(array, "pb", [(ring[i], ring[(i + 1) % size]) for i in range(size)])
 
 
 def ring_source(at, size, hops):
@@ -79,26 +80,30 @@
     p_at, k_at = lax.axis_index("pb"), lax.axis_index("ka")
     ring_at, core_at = k_at // cores, lax.rem(k_at, cores)
     scale = math.log2(math.e) / math.sqrt(HEAD_DIM)
-    class_local = held // len(places[0][0])
+    class_local = held // len(places[0][0]) // cores
     nothing = count * held
 
     def ids(where):
         found = []
-        for hops, y, c in where:
+        for hops, y in where:
             ring = lax.rem(ring_at + (rings - y), rings)
-            core = lax.rem(core_at + (cores - c), cores)
             for z in hops:
                 source = ring_source(p_at, pb, z)
-                for t in range(class_local):
-                    found.append((source * class_local + t) * ka + ring * cores + core)
+                for c in range(cores):
+                    core = lax.rem(core_at + (cores - c), cores)
+                    for t in range(class_local):
+                        found.append((source * class_local + t) * ka + ring * cores + core)
         return found
 
     def pool_from(refs_in, at, k_out, v_out):
-        for i, piece in enumerate(refs_in):
-            span = slice(at + i * held, at + (i + 1) * held)
-            k_out[span] = piece[:held]
-            v_out[span, :, :HEAD_DIM] = piece[held:]
-            v_out[span, :, HEAD_DIM:] = jnp.ones(piece[held:].shape, v_out.dtype)
+        for piece in refs_in:
+            for i in range(0, 2 * held, 2 * class_local):
+                span = slice(at, at + class_local)
+                k_out[span] = piece[i : i + class_local]
+                value = piece[i + class_local : i + 2 * class_local]
+                v_out[span, :, :HEAD_DIM] = value
+                v_out[span, :, HEAD_DIM:] = jnp.ones(value.shape, v_out.dtype)
+                at += class_local
 
     if last:
         mine = lax.rem(core_at + turned, cores) * own_slots
@@ -268,6 +273,12 @@
             copies.append(copy)
     for copy in copies:
         copy.wait()
+
+
+def merge(own_ref, other_ref, queries_ref, both_ref):
+    half = own_ref.shape[0]
+    both_ref[:half] = own_ref[...]
+    both_ref[half:] = other_ref[...]
 
 
 def fetch(cores, queries_ref, out_ref, sems):
@@ -335,33 +346,20 @@
     if cores == 2:
         starts = [starts[0], turn(starts[1], ka, cores, 0, 1)]
 
-    near = {0: starts}
-    order = [0]
-    for hop in range(1, pb // 2 + 1):
-        for z, step in ((hop, 1), (pb - hop, -1)):
-            if z not in near:
-                near[z] = [along_ring(array, pb, step) for array in near[(z - step) % pb]]
-                order.append(z)
-    staged = []
-    for stage in range(stages):
-        here = [near[z] for z in order[stage * sources : (stage + 1) * sources]]
-        if sources == 1:
-            staged.append(here[0])
-            continue
-        staged.append(
-            [
-                jnp.concatenate(
-                    [array[:class_local] for array in arrays]
-                    + [array[class_local:] for array in arrays],
-                    axis=0,
-                )
-                for arrays in zip(*here)
-            ]
-        )
+    held = cores * 2 * class_local
+    start = starts[0]
+    if cores == 2:
+        start = pl.pallas_call(
+            merge,
+            out_shape=jax.ShapeDtypeStruct((held, block_rows, head_width), keys.dtype),
+            in_specs=[vmem] * 2 + [anywhere],
+            out_specs=vmem,
+            compiler_params=pltpu.CompilerParams(vmem_limit_bytes=SMALL * 2**20),
+        )(start, starts[1], own_queries)
 
     def call(first, last, turned, pieces, places, earlier, own_queries, state, extra):
-        held = len(places) * sources * class_local
-        everything = held + len(earlier) * sources * class_local
+        held = len(places) * sources * cores * class_local
+        everything = held + len(earlier) * sources * cores * class_local
         here = own_slots if last else slots
         outs = [jax.ShapeDtypeStruct((slots, rows, 2 * HEAD_DIM), jnp.float32)]
         scratch = [
@@ -402,25 +400,41 @@
             ),
         )(table, own_queries, *pieces, *extra, *state)
 
-    placed = []
+    def along(array, count):
+        found = []
+        for _ in range(count):
+            array = along_ring(array, pb)
+            found.append(array)
+        return found
+
+    def stacked(arrays):
+        return arrays[0] if len(arrays) == 1 else jnp.concatenate(arrays, axis=0)
+
+    def beside(array):
+        found = [array]
+        for _ in range(rings - 1):
+            found.append(turn(found[-1], ka, cores, 1, 0))
+        return found
+
+    hops = [range(stage * sources, (stage + 1) * sources) for stage in range(stages)]
+    placed = [[(hops[stage], y) for y in range(rings)] for stage in range(stages)]
+    state, earlier, before = [], [], []
+    arrived = [start] + along(start, sources - 1)
+    ready = None
     for stage in range(stages):
-        hops = order[stage * sources : (stage + 1) * sources]
-        places, pieces = [], []
-        for c in range(cores):
-            ring = staged[stage][c]
-            for y in range(rings):
-                if y:
-                    ring = turn(ring, ka, cores, 1, 0)
-                places.append((hops, y, c))
-                pieces.append(ring)
-        placed.append((places, pieces))
-    state, earlier, before = [], [], []
-    for stage in range(stages - 1):
-        places, pieces = placed[stage]
-        ahead = [staged[stage + 1][-1]]
-        state = call(stage == 0, False, 0, pieces, places, earlier, own_queries, state, ahead)
-        earlier, before = earlier + places, before + pieces
-    places, pieces = placed[-1]
+        if ready is not None:
+            arrived, ready, state = lax.optimization_barrier((arrived, ready, state))
+        pieces = beside(stacked(arrived))
+        if stage < stages - 1:
+            arrived = along(arrived[-1], sources)
+        if ready is not None:
+            state = call(
+                stage == 1, False, 0, ready, placed[stage - 1], earlier, own_queries, state,
+                [pieces[0]],
+            )
+            earlier, before = earlier + placed[stage - 1], before + ready
+        ready = pieces
+    places, pieces = placed[-1], ready
     halves = []
     for c in reversed(range(cores)):
         *state, half = call(False, True, c, pieces, places, earlier, own_queries, state, before)
@@ -433,6 +447,7 @@
         in_specs=[vmem] * 2,
         out_specs=anywhere,
         scratch_shapes=[pltpu.SemaphoreType.DMA((cores, PARTS))],
+        compiler_params=pltpu.CompilerParams(vmem_limit_bytes=SMALL * 2**20),
     )(halves[1], turn(halves[0], ka, cores, 0, 1))
 
 

time: 66.5 us -> 62.3 us (0.937)
  the two profiles are of different devices: /device:TPU:9 before, /device:TPU:27 now
where the time goes in v1:
time: 62.3 us; the launch traced here: 61.8 us
  Pallas kernels  36.7 us (59%)
  waiting for transfers between devices  13.1 us (21%)
  starting transfers between devices  11.6 us (19%)
    pallas_call x5, Pallas kernels, call(): pl.pallas_call(functools.partial(attend_stage, (pb, ka, cores, places, ea...  32.6 us
    ppermute x6, waiting for transfers between devices, turn(): return lax.ppermute(array, 'ka', pairs)  10.4 us
    ppermute x6, starting transfers between devices, turn(): return lax.ppermute(array, 'ka', pairs)  8.84 us
    ppermute x3, starting transfers between devices, along_ring(): lax.ppermute(array, 'pb', [(ring[i], ring[(i + 1) % size]) for i in range...  2.76 us
    ppermute x3, waiting for transfers between devices, along_ring(): lax.ppermute(array, 'pb', [(ring[i], ring[(i + 1) % size]) for i in range...  2.67 us
    pallas_call x1, Pallas kernels, on_device(): pl.pallas_call(functools.partial(split, cores), out_shape=[part] * cores,...  1.69 us
    pallas_call x1, Pallas kernels, on_device(): pl.pallas_call(functools.partial(fetch, cores), out_shape=jax.ShapeDtypeS...  1.35 us
  transfers between devices with their start and end apart: 9, of which 6 were waited for; matrix products, arithmetic and copies ran while one was open for 0% of the time, Pallas kernels for 36%

profile of v1, /device:TPU:27, one launch (start us, length us, event | category | flops | bytes accessed | tf_op | source)
XLA Modules:
  0.0 61.8 jit_solution(12711719353311591627)
XLA Ops:
  0.0 0.0 copy-start.2
  0.0 0.0 copy-start.1
  0.0 1.7 %shard_map.56 = (bf16[4,128,128]{2,1,0:T(8,128)(2,1)}, bf16[4,128,128]{2,1,0:T(8,128)(2,1)}) custom-call(bf16[2,1,128,256]{3,2,1,0:T(8,128)(2,1)} %keys_ref.1, bf16[2,1,128,256]{3,2,1,0:T(8,128)(2,1)} %values_ref.1), custom_call_target="tpu_custom_call" | custom-call | tf_op jit(solution)/shard_map/pallas_call | solution.py:330
  1.7 0.0 copy-start
  1.7 0.7 %collective-permute-start = (bf16[4,128,128]{2,1,0:T(8,128)(2,1)}, bf16[4,128,128]{2,1,0:T(8,128)(2,1)S(1)}, u32[]{:S(2)}, u32[]{:S(2)}) collective-permute-start(bf16[4,128,128]{2,1,0:T(8,128)(2,1)} %get-tuple-element.22), channel_id=1, source_target_pairs={{0,2},{2,0},{4,6},{6,4},{1,3},{3,1},{5,7},{7,5},{8,10},{10,8},{12,... | collective-permute-start | bytes 393224 | tf_op jit(solution)/shard_map/ppermute | solution.py:43
  2.5 1.3 %shard_map.55.queries_ref.q_ref = bf16[512,1024]{1,0:T(8,128)(2,1)S(1)} custom-call(bf16[1024,2048]{1,0:T(8,128)(2,1)} %queries_ref.1), custom_call_target="tpu_custom_call" | custom-call | tf_op jit(solution)/shard_map/pallas_call | solution.py:338
  3.8 0.0 collective-permute-done.other_ref
  3.8 0.0 copy-done
  3.9 1.3 %collective-permute-start.2 = (bf16[8,128,128]{2,1,0:T(8,128)(2,1)S(1)}, bf16[8,128,128]{2,1,0:T(8,128)(2,1)S(1)}, u32[]{:S(2)}, u32[]{:S(2)}) collective-permute-start(bf16[8,128,128]{2,1,0:T(8,128)(2,1)S(1)} %shard_map.57.refs_0_.refs_2_), channel_id=1, source_target_pairs={{0,4},{2,6},{4,0},{6,2},{1,5},{3,7},{5,1},{7,3},{8,12},{10,14},{12... | collective-permute-start | bytes 786440 | tf_op jit(solution)/shard_map/ppermute | solution.py:43
  5.2 0.1 collective-permute-start.1
  5.2 0.0 copy-done.2
  5.2 0.1 copy.10
  5.3 6.4 %collective-permute-done.2.refs_1_.refs_3_ = bf16[8,128,128]{2,1,0:T(8,128)(2,1)S(1)} collective-permute-done((bf16[8,128,128]{2,1,0:T(8,128)(2,1)S(1)}, bf16[8,128,128]{2,1,0:T(8,128)(2,1)S(1)}, u32[]{:S(2)}, u32[]{:S(2)}) %collective-permute-start.2) | collective-permute-done | bytes 262176 | tf_op jit(solution)/shard_map/ppermute | solution.py:43
  11.7 0.9 %collective-permute-done.1.refs_2_.refs_0_.refs_4_ = bf16[8,128,128]{2,1,0:T(8,128)(2,1)S(1)} collective-permute-done((bf16[8,128,128]{2,1,0:T(8,128)(2,1)S(1)}, bf16[8,128,128]{2,1,0:T(8,128)(2,1)S(1)}, u32[]{:S(2)}, u32[]{:S(2)}) %collective-permute-start.1) | collective-permute-done | bytes 262176 | tf_op jit(solution)/shard_map/ppermute | solution.py:27
  12.6 0.3 collective-permute-start.4
  12.9 0.9 %collective-permute-start.3 = (bf16[8,128,128]{2,1,0:T(8,128)(2,1)S(1)}, bf16[8,128,128]{2,1,0:T(8,128)(2,1)S(1)}, u32[]{:S(2)}, u32[]{:S(2)}) collective-permute-start(bf16[8,128,128]{2,1,0:T(8,128)(2,1)S(1)} %collective-permute-done.1.refs_2_.refs_0_.refs_4_), channel_id=1, source_target_pairs={{0,16},{16,24},{24,8},{8,0},{1,17},{17,25},{25,9},{9,1},{2,18},{18... | collective-permute-start | bytes 786440 | tf_op jit(solution)/shard_map/ppermute | solution.py:27
  13.8 0.0 copy-done.1
  13.8 0.1 pad_add_fusion.table_ref
  13.8 2.0 %shard_map.58.refs_3_ = f32[4,1024,256]{2,1,0:T(8,128)S(1)} custom-call(s32[8,33]{1,0:T(8,128)S(1)} %pad_add_fusion.table_ref, bf16[512,1024]{1,0:T(8,128)(2,1)S(1)} %shard_map.55.queries_ref.q_ref, bf16[8,128,128]{2,1,0:T(8,128)(2,1)S(1)} %shard_map.57.refs_0_.refs_2_, bf16[8,128,128]{2,1,0:T(8,128)(2,1)S(1)} %collective-permute-done.2.refs_1_.refs_3_, ...), custom_call_target="tpu_custom_call" | custom-call | flops 2147483648 | bytes 4194304 | tf_op jit(solution)/shard_map/pallas_call | solution.py:381
  15.8 3.3 %collective-permute-done.4.refs_1_.refs_5_ = bf16[8,128,128]{2,1,0:T(8,128)(2,1)S(1)} collective-permute-done((bf16[8,128,128]{2,1,0:T(8,128)(2,1)S(1)}, bf16[8,128,128]{2,1,0:T(8,128)(2,1)S(1)}, u32[]{:S(2)}, u32[]{:S(2)}) %collective-permute-start.4) | collective-permute-done | bytes 262176 | tf_op jit(solution)/shard_map/ppermute | solution.py:43
  19.1 0.1 collective-permute-done.3.refs_2_.refs_0_.refs_6_
  19.2 1.0 %collective-permute-start.6 = (bf16[8,128,128]{2,1,0:T(8,128)(2,1)S(1)}, bf16[8,128,128]{2,1,0:T(8,128)(2,1)S(1)}, u32[]{:S(2)}, u32[]{:S(2)}) collective-permute-start(bf16[8,128,128]{2,1,0:T(8,128)(2,1)S(1)} %collective-permute-done.3.refs_2_.refs_0_.refs_6_), channel_id=1, source_target_pairs={{0,4},{2,6},{4,0},{6,2},{1,5},{3,7},{5,1},{7,3},{8,12},{10,14},{12... | collective-permute-start | bytes 786440 | tf_op jit(solution)/shard_map/ppermute | solution.py:43
  20.3 1.9 %collective-permute-start.5 = (bf16[8,128,128]{2,1,0:T(8,128)(2,1)S(1)}, bf16[8,128,128]{2,1,0:T(8,128)(2,1)S(1)}, u32[]{:S(2)}, u32[]{:S(2)}) collective-permute-start(bf16[8,128,128]{2,1,0:T(8,128)(2,1)S(1)} %collective-permute-done.3.refs_2_.refs_0_.refs_6_), channel_id=1, source_target_pairs={{0,16},{16,24},{24,8},{8,0},{1,17},{17,25},{25,9},{9,1},{2,18},{18... | collective-permute-start | bytes 786440 | tf_op jit(solution)/shard_map/ppermute | solution.py:27
  22.1 2.5 %shard_map.59.refs_3_ = f32[4,1024,256]{2,1,0:T(8,128)S(1)} custom-call(s32[8,33]{1,0:T(8,128)S(1)} %pad_add_fusion.table_ref, bf16[512,1024]{1,0:T(8,128)(2,1)S(1)} %shard_map.55.queries_ref.q_ref, bf16[8,128,128]{2,1,0:T(8,128)(2,1)S(1)} %collective-permute-done.1.refs_2_.refs_0_.refs_4_, ...), custom_call_target="tpu_custom_call", output_to_operand_aliasing={{}: (5, {})} | custom-call | flops 2147483648 | bytes 4194304 | tf_op jit(solution)/shard_map/pallas_call | solution.py:381
  24.7 0.0 collective-permute-done.6.refs_1_.refs_7_
  24.7 1.6 %collective-permute-done.5.refs_2_.refs_0_ = bf16[8,128,128]{2,1,0:T(8,128)(2,1)S(1)} collective-permute-done((bf16[8,128,128]{2,1,0:T(8,128)(2,1)S(1)}, bf16[8,128,128]{2,1,0:T(8,128)(2,1)S(1)}, u32[]{:S(2)}, u32[]{:S(2)}) %collective-permute-start.5) | collective-permute-done | bytes 262176 | tf_op jit(solution)/shard_map/ppermute | solution.py:27
  26.3 0.2 collective-permute-start.7
  26.5 4.2 %shard_map.60.refs_8_ = f32[4,1024,256]{2,1,0:T(8,128)S(1)} custom-call(s32[8,33]{1,0:T(8,128)S(1)} %pad_add_fusion.table_ref, bf16[512,1024]{1,0:T(8,128)(2,1)S(1)} %shard_map.55.queries_ref.q_ref, bf16[8,128,128]{2,1,0:T(8,128)(2,1)S(1)} %collective-permute-done.3.refs_2_.refs_0_.refs_6_, ...), custom_call_target="tpu_custom_call", output_to_operand_aliasing={{}: (5, {})} | custom-call | flops 2147483648 | bytes 4194304 | tf_op jit(solution)/shard_map/pallas_call | solution.py:381
  30.7 0.8 %collective-permute-done.7.refs_1_ = bf16[8,128,128]{2,1,0:T(8,128)(2,1)S(1)} collective-permute-done((bf16[8,128,128]{2,1,0:T(8,128)(2,1)S(1)}, bf16[8,128,128]{2,1,0:T(8,128)(2,1)S(1)}, u32[]{:S(2)}, u32[]{:S(2)}) %collective-permute-start.7) | collective-permute-done | bytes 262176 | tf_op jit(solution)/shard_map/ppermute | solution.py:43
  31.5 11.5 %shard_map.61 = (f32[4,1024,256]{2,1,0:T(8,128)S(1)}, bf16[256,1024]{1,0:T(8,128)(2,1)S(1)}) custom-call(s32[8,33]{1,0:T(8,128)S(1)} %pad_add_fusion.table_ref, bf16[512,1024]{1,0:T(8,128)(2,1)S(1)} %shard_map.55.queries_ref.q_ref, bf16[8,128,128]{2,1,0:T(8,128)(2,1)S(1)} %collective-permute-done.5.refs_2_.refs_0_, ...), custom_call_target="tpu_custom_call", output_to_operand_aliasing={{0}: (10, {})} | custom-call | flops 2147483648 | bytes 4194304 | tf_op jit(solution)/shard_map/pallas_call | solution.py:381
  43.0 5.2 %collective-permute-start.8 = (bf16[256,1024]{1,0:T(8,128)(2,1)S(1)}, bf16[256,1024]{1,0:T(8,128)(2,1)S(1)}, u32[]{:S(2)}, u32[]{:S(2)}) collective-permute-start(bf16[256,1024]{1,0:T(8,128)(2,1)S(1)} %get-tuple-element.36), channel_id=1, source_target_pairs={{0,2},{2,0},{4,6},{6,4},{1,3},{3,1},{5,7},{7,5},{8,10},{10,8},{12,... | collective-permute-start | bytes 1572872 | tf_op jit(solution)/shard_map/ppermute | solution.py:43
  48.2 12.3 %shard_map.62 = (f32[4,1024,256]{2,1,0:T(8,128)S(1)}, bf16[256,1024]{1,0:T(8,128)(2,1)S(1)}) custom-call(s32[8,33]{1,0:T(8,128)S(1)} %pad_add_fusion.table_ref, bf16[512,1024]{1,0:T(8,128)(2,1)S(1)} %shard_map.55.queries_ref.q_ref, bf16[8,128,128]{2,1,0:T(8,128)(2,1)S(1)} %collective-permute-done.5.refs_2_.refs_0_, ...), custom_call_target="tpu_custom_call", output_to_operand_aliasing={{0}: (10, {})} | custom-call | flops 2147483648 | bytes 4194304 | tf_op jit(solution)/shard_map/pallas_call | solution.py:381
  60.6 0.0 collective-permute-done.8.other_ref
  60.6 1.1 %shard_map.63 = bf16[256,2048]{1,0:T(8,128)(2,1)} custom-call(bf16[256,1024]{1,0:T(8,128)(2,1)S(1)} %get-tuple-element.35.own_ref, bf16[256,1024]{1,0:T(8,128)(2,1)S(1)} %collective-permute-done.8.other_ref), custom_call_target="tpu_custom_call" | custom-call | tf_op jit(solution)/shard_map/pallas_call | solution.py:444
  (1 shorter events, 0.0 us)
Async XLA Ops:
  0.0 5.2 %copy-start.2 = (s32[8]{0:T(128)S(1)}, s32[8]{0:T(128)}, u32[]{:S(2)}) copy-start(s32[8]{0:T(128)} %param.8) | copy-start | bytes 100
  0.0 13.8 %copy-start.1 = (s32[8,32]{1,0:T(8,128)S(1)}, s32[8,32]{1,0:T(8,128)}, u32[]{:S(2)}) copy-start(s32[8,32]{1,0:T(8,128)} %param.9) | copy-start | bytes 3076
  1.7 2.1 %copy-start = (bf16[4,128,128]{2,1,0:T(8,128)(2,1)S(1)}, bf16[4,128,128]{2,1,0:T(8,128)(2,1)}, u32[]{:S(2)}) copy-start(bf16[4,128,128]{2,1,0:T(8,128)(2,1)} %get-tuple-element.21.own_ref) | copy-start | bytes 393220
  1.7 2.1 %collective-permute-start = (bf16[4,128,128]{2,1,0:T(8,128)(2,1)}, bf16[4,128,128]{2,1,0:T(8,128)(2,1)S(1)}, u32[]{:S(2)}, u32[]{:S(2)}) collective-permute-start(bf16[4,128,128]{2,1,0:T(8,128)(2,1)} %get-tuple-element.22), channel_id=1, source_target_pairs={{0,2},{2,0},{4,6},{6,4},{1,3},{3,1},{5,7},{7,5},{8,10},{10,8},{12,... | collective-permute-start | bytes 393224 | tf_op jit(solution)/shard_map/ppermute | solution.py:43
  3.9 7.8 %collective-permute-start.2 = (bf16[8,128,128]{2,1,0:T(8,128)(2,1)S(1)}, bf16[8,128,128]{2,1,0:T(8,128)(2,1)S(1)}, u32[]{:S(2)}, u32[]{:S(2)}) collective-permute-start(bf16[8,128,128]{2,1,0:T(8,128)(2,1)S(1)} %shard_map.57.refs_0_.refs_2_), channel_id=1, source_target_pairs={{0,4},{2,6},{4,0},{6,2},{1,5},{3,7},{5,1},{7,3},{8,12},{10,14},{12... | collective-permute-start | bytes 786440 | tf_op jit(solution)/shard_map/ppermute | solution.py:43
  5.2 7.4 %collective-permute-start.1 = (bf16[8,128,128]{2,1,0:T(8,128)(2,1)S(1)}, bf16[8,128,128]{2,1,0:T(8,128)(2,1)S(1)}, u32[]{:S(2)}, u32[]{:S(2)}) collective-permute-start(bf16[8,128,128]{2,1,0:T(8,128)(2,1)S(1)} %shard_map.57.refs_0_.refs_2_), channel_id=1, source_target_pairs={{0,16},{16,24},{24,8},{8,0},{1,17},{17,25},{25,9},{9,1},{2,18},{18... | collective-permute-start | bytes 786440 | tf_op jit(solution)/shard_map/ppermute | solution.py:27
  12.6 6.5 %collective-permute-start.4 = (bf16[8,128,128]{2,1,0:T(8,128)(2,1)S(1)}, bf16[8,128,128]{2,1,0:T(8,128)(2,1)S(1)}, u32[]{:S(2)}, u32[]{:S(2)}) collective-permute-start(bf16[8,128,128]{2,1,0:T(8,128)(2,1)S(1)} %collective-permute-done.1.refs_2_.refs_0_.refs_4_), channel_id=1, source_target_pairs={{0,4},{2,6},{4,0},{6,2},{1,5},{3,7},{5,1},{7,3},{8,12},{10,14},{12... | collective-permute-start | bytes 786440 | tf_op jit(solution)/shard_map/ppermute | solution.py:43
  12.9 6.3 %collective-permute-start.3 = (bf16[8,128,128]{2,1,0:T(8,128)(2,1)S(1)}, bf16[8,128,128]{2,1,0:T(8,128)(2,1)S(1)}, u32[]{:S(2)}, u32[]{:S(2)}) collective-permute-start(bf16[8,128,128]{2,1,0:T(8,128)(2,1)S(1)} %collective-permute-done.1.refs_2_.refs_0_.refs_4_), channel_id=1, source_target_pairs={{0,16},{16,24},{24,8},{8,0},{1,17},{17,25},{25,9},{9,1},{2,18},{18... | collective-permute-start | bytes 786440 | tf_op jit(solution)/shard_map/ppermute | solution.py:27
  19.2 5.4 %collective-permute-start.6 = (bf16[8,128,128]{2,1,0:T(8,128)(2,1)S(1)}, bf16[8,128,128]{2,1,0:T(8,128)(2,1)S(1)}, u32[]{:S(2)}, u32[]{:S(2)}) collective-permute-start(bf16[8,128,128]{2,1,0:T(8,128)(2,1)S(1)} %collective-permute-done.3.refs_2_.refs_0_.refs_6_), channel_id=1, source_target_pairs={{0,4},{2,6},{4,0},{6,2},{1,5},{3,7},{5,1},{7,3},{8,12},{10,14},{12... | collective-permute-start | bytes 786440 | tf_op jit(solution)/shard_map/ppermute | solution.py:43
  20.3 6.0 %collective-permute-start.5 = (bf16[8,128,128]{2,1,0:T(8,128)(2,1)S(1)}, bf16[8,128,128]{2,1,0:T(8,128)(2,1)S(1)}, u32[]{:S(2)}, u32[]{:S(2)}) collective-permute-start(bf16[8,128,128]{2,1,0:T(8,128)(2,1)S(1)} %collective-permute-done.3.refs_2_.refs_0_.refs_6_), channel_id=1, source_target_pairs={{0,16},{16,24},{24,8},{8,0},{1,17},{17,25},{25,9},{9,1},{2,18},{18... | collective-permute-start | bytes 786440 | tf_op jit(solution)/shard_map/ppermute | solution.py:27
  26.3 5.2 %collective-permute-start.7 = (bf16[8,128,128]{2,1,0:T(8,128)(2,1)S(1)}, bf16[8,128,128]{2,1,0:T(8,128)(2,1)S(1)}, u32[]{:S(2)}, u32[]{:S(2)}) collective-permute-start(bf16[8,128,128]{2,1,0:T(8,128)(2,1)S(1)} %collective-permute-done.5.refs_2_.refs_0_), channel_id=1, source_target_pairs={{0,4},{2,6},{4,0},{6,2},{1,5},{3,7},{5,1},{7,3},{8,12},{10,14},{12... | collective-permute-start | bytes 786440 | tf_op jit(solution)/shard_map/ppermute | solution.py:43
  43.0 17.5 %collective-permute-start.8 = (bf16[256,1024]{1,0:T(8,128)(2,1)S(1)}, bf16[256,1024]{1,0:T(8,128)(2,1)S(1)}, u32[]{:S(2)}, u32[]{:S(2)}) collective-permute-start(bf16[256,1024]{1,0:T(8,128)(2,1)S(1)} %get-tuple-element.36), channel_id=1, source_target_pairs={{0,2},{2,0},{4,6},{6,4},{1,3},{3,1},{5,7},{7,5},{8,10},{10,8},{12,... | collective-permute-start | bytes 1572872 | tf_op jit(solution)/shard_map/ppermute | solution.py:43
